TPU v7x, 32 devices: a whole 2x2x4 slice. The times are simulated.
32 devices in a mesh: groups: 2 (over y), date: 4 (over z), pix: 2 (over x), chan: 2 (over core).
Axes of the slice: x: 2, y: 2, z: 4, core: 2. Of those that a mesh axis runs over, the one named last changes fastest.
Arguments:
- frames: bfloat16 [128, 4, 64, 128], P(('groups', 'date'), 'pix'), parts along dimension 0, may hold values from -6 to 6
- spatial_weight: bfloat16 [3, 3, 64, 64], P(None, None, None, 'chan'), may hold values from -0.25 to 0.25
- spatial_bias: float32 [64], P('chan'), may hold values from -3 to 3
- temporal_weight: bfloat16 [64, 64, 16], P('date', 'chan'), may hold values from -0.1875 to 0.1875
- temporal_bias: float32 [16], replicated, may hold values from -4 to 4
- head_weight: float32 [16], replicated, may hold values from -3 to 3
- labels: int32 [8, 128], P(('groups', 'pix'), ('date', 'chan')), parts along dimension 0, may hold values 0 or 1
Outputs:
- logits: float32 [8, 128], P(('groups', 'pix'), ('date', 'chan')), parts along dimension 0
- grad_spatial: float32 [6, 3, 64, 64], P('groups', None, None, 'chan'), parts along dimension 0
- grad_temporal: float32 [64, 64, 32], P('date', 'chan', 'groups'), parts along dimension 2
There are 2 independent parts, one for each index of `groups`. A program takes and returns all parts, laid end to end along the dimension named above; an argument that names none is the same for every part. Nothing has to cross between parts.
All inputs are finite; a program needn't handle non-finite values. No bound on the sum of `labels` on one device may be relied on, other than what follows from the above.
Results may differ from a plain program's by a relative error of at most 0.024.
Values may be sent and summed in bfloat16 or wider, within the bound.
A program may use at most 64 MiB of HBM per device.

v0:
```python
import jax
import jax.numpy as jnp
from jax import lax
from jax.sharding import PartitionSpec as P


def with_halo(block, sides, width):
    for axis, dim in sides:
        count = lax.axis_size(axis)
        forward = [(i, i + 1) for i in range(count - 1)]
        backward = [(target, source) for source, target in forward]
        low = lax.ppermute(
            lax.slice_in_dim(block, block.shape[dim] - width, None, axis=dim), axis, forward
        )
        high = lax.ppermute(lax.slice_in_dim(block, 0, width, axis=dim), axis, backward)
        block = jnp.concatenate([low, block, high], axis=dim)
    return block


def shards(
    frames, spatial_weight, spatial_bias, temporal_weight, temporal_bias, head_weight, labels
):
    dates_here, rows, channels, columns = frames.shape
    padded = with_halo(frames, (("pix", 1),), 1)
    padded = jnp.pad(padded, ((0, 0), (0, 0), (0, 0), (1, 1)))
    preact = spatial_bias[None, None, :, None]
    for row_off in range(3):
        for col_off in range(3):
            window = padded[:, row_off : row_off + rows, :, col_off : col_off + columns]
            preact = preact + jnp.einsum(
                "ticj,co->tioj",
                window,
                spatial_weight[row_off, col_off],
                preferred_element_type=jnp.float32,
            )
    sigmoid_pre = jax.nn.sigmoid(preact)
    hidden = (preact * sigmoid_pre).astype(jnp.bfloat16)
    partial_feat = jnp.einsum(
        "tioj,tof->fij", hidden, temporal_weight, preferred_element_type=jnp.float32
    )
    feature = (
        lax.psum_scatter(partial_feat, ("date", "chan"), scatter_dimension=2, tiled=True)
        + temporal_bias[:, None, None]
    )
    sigmoid_feat = jax.nn.sigmoid(feature)
    logits = jnp.einsum("fij,f->ij", feature * sigmoid_feat, head_weight)
    dlogit = jax.nn.sigmoid(logits) - labels.astype(jnp.float32)
    feature_grad = (
        dlogit[None]
        * head_weight[:, None, None]
        * sigmoid_feat
        * (1.0 + feature * (1.0 - sigmoid_feat))
    ).astype(jnp.bfloat16)
    full_grad = lax.all_gather(feature_grad, ("date", "chan"), axis=2, tiled=True)
    temporal_part = jnp.einsum(
        "tioj,fij->tof", hidden, full_grad, preferred_element_type=jnp.float32
    )
    hidden_grad = jnp.einsum(
        "fij,tof->tioj", full_grad, temporal_weight, preferred_element_type=jnp.float32
    )
    preact_grad = (hidden_grad * sigmoid_pre * (1.0 + preact * (1.0 - sigmoid_pre))).astype(
        jnp.bfloat16
    )
    rows_out = []
    for row_off in range(3):
        cols_out = []
        for col_off in range(3):
            window = padded[:, row_off : row_off + rows, :, col_off : col_off + columns]
            cols_out.append(
                jnp.einsum("ticj,tioj->co", window, preact_grad, preferred_element_type=jnp.float32)
            )
        rows_out.append(jnp.stack(cols_out))
    spatial_part = jnp.stack(rows_out)
    grad_temporal = lax.psum(temporal_part, "pix")
    grad_spatial = lax.psum(spatial_part, ("date", "pix"))
    return (logits, grad_spatial, grad_temporal)


def solution(mesh):
    placed = (
        P(("groups", "date"), "pix", None, None),
        P(None, None, None, "chan"),
        P("chan"),
        P("date", "chan", None),
        P(),
        P(),
        P(("groups", "pix"), ("date", "chan")),
    )
    return jax.shard_map(
        shards,
        mesh=mesh,
        in_specs=placed,
        out_specs=(
            P(("groups", "pix"), ("date", "chan")),
            P("groups", None, None, "chan"),
            P("date", "chan", "groups"),
        ),
        check_vma=False,
    )
```

profile of v0, /device:TPU:0, one launch (start us, length us, event | category | flops | bytes accessed | tf_op | source)
XLA Modules:
  0.0 157.4 jit_solution(17748076628413484052)
XLA Ops:
  7.2 1.1 fusion.79
  8.4 4.9 %collective-permute-start = (bf16[16,1,64,128]{3,2,1,0:T(8,128)(2,1)S(1)}, bf16[16,1,64,128]{3,2,1,0:T(8,128)(2,1)S(1)}, u32[]{:S(2)}, u32[]{:S(2)}) collective-permute-start(bf16[16,1,64,128]{3,2,1,0:T(8,128)(2,1)S(1)} %get-tuple-element.11), channel_id=1, source_target_pairs={{0,2},{1,3},{4,6},{5,7},{8,10},{9,11},{12,14},{13,15},{16,18},{17,... | collective-permute-start | bytes 786440 | tf_op jit(solution)/shard_map/ppermute | solution.py:12
  13.3 1.4 collective-permute-start.1
  14.7 1.3 fusion.47
  16.0 2.8 %collective-permute-done = bf16[16,1,64,128]{3,2,1,0:T(8,128)(2,1)S(1)} collective-permute-done((bf16[16,1,64,128]{3,2,1,0:T(8,128)(2,1)S(1)}, bf16[16,1,64,128]{3,2,1,0:T(8,128)(2,1)S(1)}, u32[]{:S(2)}, u32[]{:S(2)}) %collective-permute-start) | collective-permute-done | bytes 262176 | tf_op jit(solution)/shard_map/ppermute | solution.py:12
  18.8 4.3 %collective-permute-done.1 = bf16[16,1,64,128]{3,2,1,0:T(8,128)(2,1)S(1)} collective-permute-done((bf16[16,1,64,128]{3,2,1,0:T(8,128)(2,1)S(1)}, bf16[16,1,64,128]{3,2,1,0:T(8,128)(2,1)S(1)}, u32[]{:S(2)}, u32[]{:S(2)}) %collective-permute-start.1) | collective-permute-done | bytes 262176 | tf_op jit(solution)/shard_map/ppermute | solution.py:15
  23.0 1.1 fusion.5
  24.2 0.4 fusion.40
  24.5 0.4 fusion.51
  26.0 0.2 fusion.15
  26.2 1.2 multiply_convert_fusion
  27.6 0.8 copy.76
  28.4 1.7 %reshape.35 = f32[128,32]{1,0:T(8,128)} reshape(f32[128,2,16]{2,1,0:T(2,128)} %bitcast.179) | data formatting | bytes 32768
  30.2 2.2 %fusion.78 = (bf16[16,2,64,128]{3,2,1,0:T(8,128)(2,1)}, bf16[16,2,64,128]{3,2,1,0:T(8,128)(2,1)}, bf16[16,2,64,128]{3,2,1,0:T(8,128)(2,1)}, bf16[16,2,64,128]{3,...) fusion(bf16[16,4,64,130]{3,2,1,0:T(8,128)(2,1)S(1)} %fusion.5), kind=kLoop, calls=%fused_computation.104 | loop fusion | bytes 6291456 | tf_op jit(solution)/shard_map/slice | solution.py:29
  32.4 28.2 %reduce-scatter.4.cloned.1.call-done = f32[16,32]{1,0:T(8,128)} async-done(((f32[128,32]{1,0:T(8,128)}), f32[16,32]{1,0:T(8,128)}) %reduce-scatter.4.cloned.1.call-update) | async-done | bytes 2064
  60.6 0.8 reshape.36
  61.9 14.0 %all_gather.3 = bf16[16,2,128]{0,1,2:T(2,128)(2,1)S(1)} all-gather(bf16[16,2,16]{0,1,2:T(2,128)(2,1)S(1)} %copy.31), channel_id=1, replica_groups=mesh['groups'=2,'date'=4,'pix'=2,'chan'=2] {'date','chan'}, dimensions={2}, use_global_device_ids=true | all-gather | bytes 9216 | tf_op jit(solution)/shard_map/all_gather | solution.py:54
  75.9 1.4 fusion.16
  77.3 0.3 convolution_bitcast_fusion.10
  77.6 0.3 convolution_bitcast_fusion.4
  77.9 0.3 convolution_bitcast_fusion.7
  78.4 0.3 convolution_bitcast_fusion.11
  78.6 0.3 convolution_bitcast_fusion.5
  78.9 0.3 convolution_bitcast_fusion.6
  79.2 0.3 convolution_bitcast_fusion.8
  79.4 0.3 convolution_bitcast_fusion.9
  79.8 0.3 convolution_bitcast_fusion.3
  80.1 0.7 pad_maximum_fusion.2
  80.8 0.3 convolution_bitcast_fusion.1
  81.0 10.8 %psum.15 = f32[16,32,16]{1,2,0:T(8,128)} all-reduce(f32[16,32,16]{1,2,0:T(8,128)S(1)} %convolution_bitcast_fusion.1), channel_id=1, replica_groups=mesh['groups'=2,'date'=4,'pix'=2,'chan'=2] {'pix'}, use_global_device_ids=true, to_apply=%region_2.3 | all-reduce | flops 8192 | bytes 65536 | tf_op jit(solution)/shard_map/psum | solution.py:74
  91.8 57.2 %all-reduce.3.cloned.1.call-done = f32[3,3,64,32]{2,3,1,0:T(8,128)} async-done(((f32[3,3,64,32]{2,3,1,0:T(8,128)}), f32[3,3,64,32]{2,3,1,0:T(8,128)}) %all-reduce.3.cloned.1.call-update) | async-done | bytes 73744 | tf_op jit(solution)/shard_map/psum | solution.py:75
  149.0 1.6 %copy.115 = f32[3,3,64,32]{2,3,1,0:T(8,128)} copy(f32[3,3,64,32]{2,3,1,0:T(8,128)} %all-reduce.3.cloned.1.call-done) | data formatting | bytes 147456
  (50 shorter events, 2.3 us)
Async XLA Ops:
  7.2 20.3 %copy-start = (bf16[16,32,16]{1,2,0:T(8,128)(2,1)S(1)}, bf16[16,32,16]{1,2,0:T(8,128)(2,1)}, u32[]{:S(2)}) copy-start(bf16[16,32,16]{1,2,0:T(8,128)(2,1)} %param.10) | copy-start | bytes 49156
  7.2 15.9 %copy-start.1 = (bf16[16,2,64,128]{3,2,1,0:T(8,128)(2,1)S(1)}, bf16[16,2,64,128]{3,2,1,0:T(8,128)(2,1)}, u32[]{:S(2)}) copy-start(bf16[16,2,64,128]{3,2,1,0:T(8,128)(2,1)} %param.7) | copy-start | bytes 1572868
  7.2 53.4 %reduce-scatter.4.cloned.1.call-start = ((), (), s32[]{:S(2)}) async-start(), calls=%async_computation.2 | async-start | bytes 73728
  8.4 10.4 %collective-permute-start = (bf16[16,1,64,128]{3,2,1,0:T(8,128)(2,1)S(1)}, bf16[16,1,64,128]{3,2,1,0:T(8,128)(2,1)S(1)}, u32[]{:S(2)}, u32[]{:S(2)}) collective-permute-start(bf16[16,1,64,128]{3,2,1,0:T(8,128)(2,1)S(1)} %get-tuple-element.11), channel_id=1, source_target_pairs={{0,2},{1,3},{4,6},{5,7},{8,10},{9,11},{12,14},{13,15},{16,18},{17,... | collective-permute-start | bytes 786440 | tf_op jit(solution)/shard_map/ppermute | solution.py:12
  13.2 10.9 %copy-start.10 = (bf16[3,3,64,32]{2,3,1,0:T(8,128)(2,1)S(1)}, bf16[3,3,64,32]{2,3,1,0:T(8,128)(2,1)}, u32[]{:S(2)}) copy-start(bf16[3,3,64,32]{2,3,1,0:T(8,128)(2,1)} %param.8) | copy-start | bytes 110596
  13.3 9.8 %collective-permute-start.1 = (bf16[16,1,64,128]{3,2,1,0:T(8,128)(2,1)S(1)}, bf16[16,1,64,128]{3,2,1,0:T(8,128)(2,1)S(1)}, u32[]{:S(2)}, u32[]{:S(2)}) collective-permute-start(bf16[16,1,64,128]{3,2,1,0:T(8,128)(2,1)S(1)} %get-tuple-element.12), channel_id=1, source_target_pairs={{2,0},{3,1},{6,4},{7,5},{10,8},{11,9},{14,12},{15,13},{18,16},{19,... | collective-permute-start | bytes 786440 | tf_op jit(solution)/shard_map/ppermute | solution.py:15
  25.3 0.7 copy-start.15
  25.4 0.8 copy-start.2
  30.1 31.4 %copy-start.13 = (f32[16]{0:T(128)S(1)}, f32[16]{0:T(128)}, u32[]{:S(2)}) copy-start(f32[16]{0:T(128)} %param.11) | copy-start | bytes 196
  30.1 31.4 %copy-start.14 = (f32[16]{0:T(128)S(1)}, f32[16]{0:T(128)}, u32[]{:S(2)}) copy-start(f32[16]{0:T(128)} %param.12) | copy-start | bytes 196
  30.1 31.5 %copy-start.11 = (s32[2,16]{1,0:T(2,128)S(1)}, s32[2,16]{1,0:T(2,128)}, u32[]{:S(2)}) copy-start(s32[2,16]{1,0:T(2,128)} %param.13) | copy-start | bytes 388
  30.1 118.9 %all-reduce.3.cloned.1.call-start = ((), (), s32[]{:S(2)}) async-start(), calls=%async_computation.1 | async-start | bytes 294912 | tf_op jit(solution)/shard_map/psum | solution.py:75
  32.4 44.9 %copy-start.3 = (bf16[16,2,64,128]{3,2,1,0:T(8,128)(2,1)S(1)}, bf16[16,2,64,128]{3,2,1,0:T(8,128)(2,1)}, u32[]{:S(2)}) copy-start(bf16[16,2,64,128]{3,2,1,0:T(8,128)(2,1)} %copy-done.2) | copy-start | bytes 1572868
  61.6 16.2 %copy-start.12 = (f32[1,2,16]{2,0,1:T(1,128)}, f32[1,2,16]{2,0,1:T(1,128)S(1)}, u32[]{:S(2)}) copy-start(f32[1,2,16]{2,0,1:T(1,128)S(1)} %fusion.28) | copy-start | bytes 388
  77.3 1.0 copy-start.9
  77.3 1.3 copy-start.8
  77.6 1.3 copy-start.7
  77.9 1.3 copy-start.6
  78.1 1.3 copy-start.5
  78.6 1.2 copy-start.4
Sparse Core Ops, SparseCore 0:
  30.2 30.3 reduce-scatter.3
  80.9 68.0 all-reduce.2
where the time goes:
time: 158 us; the launch traced here: 157 us
  waiting for transfers between devices  92.5 us (59%)
  blocking collectives  24.7 us (16%)
  between operations  14.3 us (9%)
  local copies, waits for them, and re-layouts  8.89 us (6%)
  matrix products  8.7 us (6%)
  starting transfers between devices  6.36 us (4%)
  other arithmetic  1.98 us (1%)
    psum x1, waiting for transfers between devices, shards(): grad_spatial = lax.psum(spatial_part, ('date', 'pix'))  57.2 us
    unnamed x3, waiting for transfers between devices  28.2 us
    all_gather x1, blocking collectives, shards(): lax.all_gather(feature_grad, ('date', 'chan'), axis=2, tiled=True)  14 us
    psum x1, blocking collectives, shards(): grad_temporal = lax.psum(temporal_part, 'pix')  10.8 us
    unnamed x37, local copies, waits for them, and re-layouts  5.36 us
    ppermute x1, starting transfers between devices, with_halo(): lax.ppermute(lax.slice_in_dim(block, block.shape[dim] - width, None, axis...  4.86 us
    ppermute x1, waiting for transfers between devices, with_halo(): lax.ppermute(lax.slice_in_dim(block, 0, width, axis=dim), axis, backward)  4.27 us
    dot_general x9, matrix products, shards(): jnp.einsum('ticj,co->tioj', window, spatial_weight[row_off, col_off], pre...  4.27 us
  transfers between devices with their start and end apart: 4, of which 4 were waited for; matrix products, arithmetic and copies ran while one was open for 2% of the time, Pallas kernels for 0%

commit v1 on v0

--- a/solution.py
+++ b/solution.py
@@ -1,7 +1,327 @@
+import functools
+
 import jax
 import jax.numpy as jnp
 from jax import lax
+from jax.experimental import pallas as pl
+from jax.experimental.pallas import tpu as pltpu
 from jax.sharding import PartitionSpec as P
+
+MESH = pl.DeviceIdType.MESH
+CHUNK = 2
+PIECE = 32
+
+
+def fused(
+    dates_n, chan_n, frames, sw, sb, tw, tb, hw, labels, logits_out, gs_out, gt_out,
+    xpad, sw_v, sb_v, tw_v, tb_v, hw_v, lab_v, wbig, hid, dact, gsh,
+    lab_all, feat_all, gt_all, dwb, rs_all, ag_all,
+    loc_sem, halo_send, halo_recv, fwd_send, fwd_recv, lab_send, lab_recv, feat_send, feat_recv,
+    gt_send, gt_recv, rs_send, rs_recv, ag_send, ag_recv,
+):
+    f32, bf16 = jnp.float32, jnp.bfloat16
+    dates, _, channels, cols = frames.shape
+    outs = sw.shape[3]
+    feats = tw.shape[2]
+    half = dates // chan_n
+    d, p, c = lax.axis_index("date"), lax.axis_index("pix"), lax.axis_index("chan")
+
+    def target(od, op, oc):
+        return {
+            "date": lax.rem(d + od, dates_n),
+            "pix": lax.rem(p + op, 2),
+            "chan": lax.rem(c + oc, chan_n),
+        }
+
+    def remote(src, dst, send, recv, where):
+        return pltpu.make_async_remote_copy(
+            src_ref=src, dst_ref=dst, send_sem=send, recv_sem=recv, device_id=where, device_id_type=MESH
+        )
+
+    barrier = pltpu.get_barrier_semaphore()
+    partners = [
+        (od, op, oc)
+        for od in range(dates_n)
+        for op in range(2)
+        for oc in range(chan_n)
+        if (od or op or oc) and not (op and oc)
+    ]
+    for offs in partners:
+        pl.semaphore_signal(barrier, inc=1, device_id=target(*offs), device_id_type=MESH)
+
+    loads = [
+        pltpu.make_async_copy(src, dst, loc_sem.at[i])
+        for i, (src, dst) in enumerate(
+            [
+                (frames, xpad.at[:, pl.ds(1, 2)]),
+                (sw, sw_v),
+                (sb, sb_v),
+                (tw, tw_v),
+                (tb, tb_v),
+                (hw, hw_v),
+                (labels, lab_v),
+            ]
+        )
+    ]
+    for load in loads:
+        load.start()
+    pl.semaphore_wait(barrier, len(partners))
+
+    halo, passed = [], []
+    for k in range(half // CHUNK):
+        mine = pl.ds(c * half + k * CHUNK, CHUNK)
+        halo.append(
+            remote(
+                frames.at[mine, 1 - p], xpad.at[mine, 3 * p], halo_send.at[k], halo_recv.at[k], target(0, 1, 0)
+            )
+        )
+        edge = xpad.at[mine, 3 - 3 * p]
+        passed.append(remote(edge, edge, fwd_send.at[k], fwd_recv.at[k], target(0, 0, 1)))
+        halo[k].start()
+
+    block = d * chan_n + c
+    width = lab_v.shape[1]
+    blocks = dates_n * chan_n
+    group = [(od, oc) for od in reversed(range(dates_n)) for oc in reversed(range(chan_n)) if od or oc]
+    loads[6].wait()
+    lane = lax.broadcasted_iota(jnp.int32, (2, cols), 1)
+    inside = (lane >= block * width) & (lane < (block + 1) * width)
+    spread = jnp.concatenate([lab_v[...].astype(f32)] * blocks, axis=1)
+    lab_all[block] = jnp.concatenate([jnp.where(inside, spread, 0.0), jnp.zeros((6, cols), f32)], axis=0)
+    lab_copies = [
+        remote(lab_all.at[block], lab_all.at[block], lab_send.at[n], lab_recv.at[n], target(od, 0, oc))
+        for n, (od, oc) in enumerate(group)
+    ]
+    for copy in lab_copies:
+        copy.start()
+
+    xpad[:, 3 * p] = jnp.zeros((dates, channels, cols), bf16)
+    gsh[...] = jnp.zeros(gsh.shape, bf16)
+    for n in range(1, 6):
+        loads[n].wait()
+    wbig[...] = jnp.zeros(wbig.shape, f32)
+    for a in range(3):
+        for b in range(3):
+            tap = sw_v[a, b].astype(f32).T
+            for i in range(2):
+                r = i + a
+                wbig[(i * 3 + b) * outs : (i * 3 + b + 1) * outs, r * channels : (r + 1) * channels] = tap
+    conv = wbig[...].astype(bf16)
+    def column(row, n):
+        same = lax.broadcasted_iota(jnp.int32, (n, n), 0) == lax.broadcasted_iota(jnp.int32, (n, n), 1)
+        return jnp.sum(jnp.where(same, row, 0.0), axis=1, keepdims=True)
+    bias_o = column(sb_v[...], outs)
+    bias_f = column(tb_v[...], feats)
+    head = column(hw_v[...], feats)
+    tw_m = tw_v[...].reshape(dates * outs, feats)
+    tw_t = tw_m.astype(f32).T.astype(bf16)
+    lane_o = lax.broadcasted_iota(jnp.int32, (outs, cols), 1)
+    first, last = lane_o == 0, lane_o == cols - 1
+
+    def right(x):
+        return jnp.where(first, 0.0, pltpu.roll(x, 1, 1))
+
+    def left(x):
+        return jnp.where(last, 0.0, pltpu.roll(x, cols - 1, 1))
+
+    def forward(start):
+        x = xpad[pl.ds(start, CHUNK)].reshape(CHUNK, 4 * channels, cols)
+        z = jnp.dot(
+            conv, jnp.concatenate([x[n] for n in range(CHUNK)], axis=1), preferred_element_type=f32
+        )
+        for n in range(CHUNK):
+            for i in range(2):
+                tap = [
+                    z[(i * 3 + b) * outs : (i * 3 + b + 1) * outs, n * cols : (n + 1) * cols] for b in range(3)
+                ]
+                pre = tap[1] + right(tap[0]) + left(tap[2]) + bias_o
+                sig = jax.nn.sigmoid(pre)
+                hid[i, start + n] = (pre * sig).astype(bf16)
+                dact[i, start + n] = sig * (1.0 + pre * (1.0 - sig))
+
+    loads[0].wait()
+    other = 1 - c
+    steps = half // CHUNK
+    for k in range(steps):
+        halo[k].wait_recv()
+        passed[k].start()
+        forward(c * half + k * CHUNK)
+        if k:
+            passed[k - 1].wait_recv()
+            forward(other * half + (k - 1) * CHUNK)
+    passed[steps - 1].wait_recv()
+    forward(other * half + (steps - 1) * CHUNK)
+
+    hid_m = [hid[i].reshape(dates * outs, cols) for i in range(2)]
+    part = jnp.concatenate([jnp.dot(tw_t, hid_m[i], preferred_element_type=f32) for i in range(2)], axis=0)
+    feat_all[block] = part.astype(bf16)
+    feat_copies = [
+        remote(feat_all.at[block], feat_all.at[block], feat_send.at[n], feat_recv.at[n], target(od, 0, oc))
+        for n, (od, oc) in enumerate(group)
+    ]
+    for copy in feat_copies:
+        copy.start()
+    for copy in lab_copies:
+        copy.wait_recv()
+    lab = jnp.sum(lab_all[...], axis=0)
+    for copy in feat_copies:
+        copy.wait_recv()
+    total = jnp.sum(feat_all[...].astype(f32), axis=0)
+
+    grads, rows_out = [], []
+    for i in range(2):
+        feature = total[i * feats : (i + 1) * feats] + bias_f
+        sig = jax.nn.sigmoid(feature)
+        logit = jnp.sum(feature * sig * head, axis=0, keepdims=True)
+        dlogit = jax.nn.sigmoid(logit) - lab[i : i + 1]
+        rows_out.append(logit)
+        grads.append((dlogit * head * sig * (1.0 + feature * (1.0 - sig))).astype(bf16))
+    fgrad = jnp.concatenate(grads, axis=1)
+
+    contract = (((1,), (1,)), ((), ()))
+    gt_all[p] = lax.dot_general(
+        fgrad, jnp.concatenate(hid_m, axis=1), contract, preferred_element_type=f32
+    )
+    gt_copy = remote(gt_all.at[p], gt_all.at[p], gt_send, gt_recv, target(0, 1, 0))
+    gt_copy.start()
+
+    for t in range(0, dates, CHUNK):
+        hgrad = jnp.dot(
+            tw_m[t * outs : (t + CHUNK) * outs], fgrad, preferred_element_type=f32
+        )
+        for n in range(CHUNK):
+            for i in range(2):
+                g = hgrad[n * outs : (n + 1) * outs, i * cols : (i + 1) * cols] * dact[i, t + n]
+                g = g.astype(bf16).astype(f32)
+                at = slice((t + n) * cols, (t + n + 1) * cols)
+                for b, v in enumerate((left(g), g, right(g))):
+                    row = i * 128 + b * outs
+                    gsh[row : row + outs, at] = v.astype(bf16)
+    x_all = jnp.concatenate(
+        [xpad[t].reshape(4 * channels, cols) for t in range(dates)], axis=1
+    )
+    dt = lax.dot_general(x_all, gsh[...], contract, preferred_element_type=f32)
+    dwb[...] = (dt[: 3 * channels, :128] + dt[channels:, 128:]).astype(bf16)
+
+    idx = d * 2 + p
+    sums = dates_n * 2
+    owners = 3 * channels // PIECE
+    shift = (sums - owners) // 2
+    mine = idx - shift
+    is_owner = (mine >= 0) & (mine < owners)
+
+    def rs_copy(k):
+        to = {"date": (k + shift) // 2, "pix": (k + shift) % 2, "chan": c}
+        return remote(
+            dwb.at[pl.ds(k * PIECE, PIECE)], rs_all.at[idx], rs_send.at[k], rs_recv.at[idx], to
+        )
+
+    for k in range(owners):
+        @pl.when(mine != k)
+        def _():
+            rs_copy(k).start()
+
+    all_other = [(od, op) for od in reversed(range(dates_n)) for op in reversed(range(2)) if od or op]
+
+    def ag_copies():
+        return [
+            remote(ag_all.at[mine], ag_all.at[mine], ag_send.at[n], ag_recv.at[mine], target(od, op, 0))
+            for n, (od, op) in enumerate(all_other)
+        ]
+
+    @pl.when(is_owner)
+    def _():
+        rs_all[idx] = dwb[pl.ds(pl.multiple_of(mine * PIECE, PIECE), PIECE)]
+        for q in range(sums):
+            @pl.when(idx != q)
+            def _():
+                pltpu.make_async_copy(rs_all.at[q], rs_all.at[q], rs_recv.at[q]).wait()
+        ag_all[mine] = jnp.sum(rs_all[...].astype(f32), axis=0).astype(bf16)
+        for copy in ag_copies():
+            copy.start()
+
+    gt_copy.wait_recv()
+    gt_out[...] = gt_all[0] + gt_all[1]
+    logit_rows = jnp.concatenate(rows_out + [jnp.zeros((6, cols), f32)], axis=0)
+    moved = pltpu.roll(logit_rows, lax.rem(cols - block * width, cols), 1)
+    logits_out[...] = moved[:2, :width]
+    for copy in halo + passed + lab_copies + feat_copies + [gt_copy]:
+        copy.wait_send()
+    for k in range(owners):
+        @pl.when(mine != k)
+        def _():
+            rs_copy(k).wait_send()
+
+    for k in range(owners):
+        @pl.when(mine != k)
+        def _():
+            pltpu.make_async_copy(ag_all.at[k], ag_all.at[k], ag_recv.at[k]).wait()
+        gs_out[k * PIECE : (k + 1) * PIECE] = ag_all[k].astype(f32)
+
+    @pl.when(is_owner)
+    def _():
+        for copy in ag_copies():
+            copy.wait_send()
+
+
+def fused_shards(dates_n, chan_n, frames, sw, sb, tw, tb, hw, labels):
+    dates, rows, channels, cols = frames.shape
+    outs, feats = sw.shape[3], tw.shape[2]
+    f32, bf16 = jnp.float32, jnp.bfloat16
+    steps = dates // chan_n // CHUNK
+    blocks, sums = dates_n * chan_n, dates_n * 2
+    owners = 3 * channels // PIECE
+    dma = pltpu.SemaphoreType.DMA
+    logits, gs, gt = pl.pallas_call(
+        functools.partial(fused, dates_n, chan_n),
+        out_shape=(
+            jax.ShapeDtypeStruct(labels.shape, f32),
+            jax.ShapeDtypeStruct((3 * channels, 128), f32),
+            jax.ShapeDtypeStruct((feats, dates * outs), f32),
+        ),
+        in_specs=[pl.BlockSpec(memory_space=pl.ANY)] * 7,
+        out_specs=[pl.BlockSpec(memory_space=pltpu.VMEM)] * 3,
+        scratch_shapes=[
+            pltpu.VMEM((dates, 4, channels, cols), bf16),
+            pltpu.VMEM(sw.shape, bf16),
+            pltpu.VMEM((1, outs), f32),
+            pltpu.VMEM(tw.shape, bf16),
+            pltpu.VMEM((1, feats), f32),
+            pltpu.VMEM((1, feats), f32),
+            pltpu.VMEM(labels.shape, jnp.int32),
+            pltpu.VMEM((6 * outs, 4 * channels), f32),
+            pltpu.VMEM((2, dates, outs, cols), bf16),
+            pltpu.VMEM((2, dates, outs, cols), f32),
+            pltpu.VMEM((256, dates * cols), bf16),
+            pltpu.VMEM((blocks, 8, cols), f32),
+            pltpu.VMEM((blocks, 2 * feats, cols), bf16),
+            pltpu.VMEM((2, feats, dates * outs), f32),
+            pltpu.VMEM((3 * channels, 128), bf16),
+            pltpu.VMEM((sums, PIECE, 128), bf16),
+            pltpu.VMEM((owners, PIECE, 128), bf16),
+            dma((7,)),
+            dma((steps,)),
+            dma((steps,)),
+            dma((steps,)),
+            dma((steps,)),
+            dma((blocks,)),
+            dma((blocks,)),
+            dma((blocks,)),
+            dma((blocks,)),
+            dma,
+            dma,
+            dma((owners,)),
+            dma((sums,)),
+            dma((sums,)),
+            dma((owners,)),
+        ],
+        compiler_params=pltpu.CompilerParams(
+            collective_id=0, has_side_effects=True, vmem_limit_bytes=40 * 1024 * 1024
+        ),
+    )(frames, sw, sb[None], tw, tb[None], hw[None], labels)
+    grad_spatial = gs[:, : 3 * outs].reshape(3, channels, 3, outs).transpose(0, 2, 1, 3)
+    grad_temporal = gt.T.reshape(dates, outs, feats)
+    return logits, grad_spatial, grad_temporal
 
 
 def with_halo(block, sides, width):
@@ -86,8 +406,12 @@
         P(),
         P(("groups", "pix"), ("date", "chan")),
     )
+    sizes = mesh.shape
+    body = shards
+    if sizes["pix"] == 2 and sizes["chan"] == 2 and sizes["date"] == 4:
+        body = functools.partial(fused_shards, sizes["date"], sizes["chan"])
     return jax.shard_map(
-        shards,
+        body,
         mesh=mesh,
         in_specs=placed,
         out_specs=(

time: 158 us -> 31 us (0.20)
  waiting for transfers between devices: 92.5 us -> 0 us
  Pallas kernels: 0 us -> 25.1 us
  blocking collectives: 24.7 us -> 0 us
  between operations: 14.3 us -> 0.72 us
  matrix products: 8.7 us -> 0 us
  starting transfers between devices: 6.36 us -> 0 us
  local copies, waits for them, and re-layouts: 8.89 us -> 4.93 us
  other arithmetic: 1.98 us -> 0 us
    psum x1 -> x0, waiting for transfers between devices: 57.2 us -> none  [shards(): grad_spatial = lax.psum(spatial_part, ('date', 'pix'))]
    unnamed x3 -> x0, waiting for transfers between devices: 28.2 us -> none
    pallas_call x0 -> x1, Pallas kernels: none -> 25.1 us  [fused_shards(): pl.pallas_call(functools.partial(fused, dates_n, chan_n), out_shape=(jax....]
    all_gather x1 -> x0, blocking collectives: 14 us -> none  [shards(): lax.all_gather(feature_grad, ('date', 'chan'), axis=2, tiled=True)]
    psum x1 -> x0, blocking collectives: 10.8 us -> none  [shards(): grad_temporal = lax.psum(temporal_part, 'pix')]
    dot_general x22 -> x0, matrix products: 8.7 us -> none  [the longest x9 4.27 us: shards(): jnp.einsum('ticj,co->tioj', window, spatial_weight[row_off, col_off], pre...]
    ppermute x2 -> x0, waiting for transfers between devices: 7.09 us -> none  [the longest x1 4.27 us: with_halo(): lax.ppermute(lax.slice_in_dim(block, 0, width, axis=dim), axis, backward)]
    ppermute x2 -> x0, starting transfers between devices: 6.28 us -> none  [the longest x1 4.86 us: with_halo(): lax.ppermute(lax.slice_in_dim(block, block.shape[dim] - width, None, axis...]
  transfers between devices with their start and end apart: 4 -> 0, of which waited for: 4 -> 0; matrix products, arithmetic and copies ran while one was open for 2% -> 0% of each run, Pallas kernels for 0% -> 0%
where the time goes in v1:
time: 31 us; the launch traced here: 30.8 us
  Pallas kernels  25.1 us (81%)
  local copies, waits for them, and re-layouts  4.93 us (16%)
  between operations  0.72 us (2%)
    pallas_call x1, Pallas kernels, fused_shards(): pl.pallas_call(functools.partial(fused, dates_n, chan_n), out_shape=(jax....  25.1 us
    unnamed x17, local copies, waits for them, and re-layouts  4.64 us

profile of v1, /device:TPU:0, one launch (start us, length us, event | category | flops | bytes accessed | tf_op | source)
XLA Modules:
  0.0 30.8 jit_solution(12156878745189863772)
XLA Ops:
  0.6 0.0 copy-start.5
  0.6 1.0 %copy.15.tw = bf16[16,32,16]{2,1,0:T(8,128)(2,1)S(1)} copy(bf16[16,32,16]{1,2,0:T(8,128)(2,1)} %param.10) | data formatting | bytes 32768 | tf_op args[3]
  1.6 0.0 copy-done.5
  1.6 0.0 copy-start.1
  1.7 0.0 copy-start.2
  1.7 0.0 copy-start.3
  1.7 0.0 copy-start.4
  1.7 0.1 copy.14.sw
  1.8 0.5 %copy-done.1 = s32[2,16]{1,0:T(2,128)S(1)} copy-done((s32[2,16]{1,0:T(2,128)S(1)}, s32[2,16]{1,0:T(2,128)}, u32[]{:S(2)}) %copy-start.1) | copy-done | bytes 152
  2.3 0.0 copy-done.2
  2.3 0.0 copy-done.3
  2.3 0.0 copy-done.4
  2.3 0.0 copy-start
  2.3 1.0 %copy-done = bf16[16,2,64,128]{3,2,1,0:T(8,128)(2,1)S(1)} copy-done((bf16[16,2,64,128]{3,2,1,0:T(8,128)(2,1)S(1)}, bf16[16,2,64,128]{3,2,1,0:T(8,128)(2,1)}, u32[]{:S(2)}) %copy-start) | copy-done | bytes 524312
  3.4 25.1 %shard_map.94 = (f32[2,16]{1,0:T(2,128)S(1)}, f32[192,128]{1,0:T(8,128)S(1)}, f32[16,512]{1,0:T(8,128)S(1)}) custom-call(bf16[16,2,64,128]{3,2,1,0:T(8,128)(2,1)S(1)} %copy-done, bf16[3,3,64,32]{3,2,1,0:T(8,128)(2,1)S(1)} %copy.14.sw, f32[1,32]{1,0:T(1,128)S(1)} %bitcast.12, bf16[16,32,16]{2,1,0:T(8,128)(2,1)S(1)} %copy.15.tw, f32[1,16]{1,0:T(1,128)S(1)} %bitcast.13, ...), custom_call_target="tpu_custom_call" | custom-call | tf_op jit(solution)/shard_map/pallas_call | solution.py:275
  28.5 0.1 copy.16
  28.6 0.1 reshape.12
  28.7 0.7 %copy.17 = f32[3,3,64,32]{2,3,1,0:T(8,128)} copy(f32[3,3,64,32]{2,0,3,1:T(4,128)S(1)} %bitcast.15) | data formatting | bytes 147456
  29.4 0.1 reshape.13
  29.5 0.7 %copy.18 = f32[16,32,16]{1,2,0:T(8,128)} copy(f32[16,32,16]{1,0,2:T(8,128)S(1)} %reshape.13) | data formatting | bytes 65536
  30.2 0.6 %copy.20 = f32[2,16]{1,0:T(2,128)} copy(f32[2,16]{1,0:T(2,128)S(1)} %get-tuple-element.18) | data formatting | bytes 256
Async XLA Ops:
  0.6 1.0 %copy-start.5 = (bf16[3,3,64,32]{2,3,1,0:T(8,128)(2,1)S(1)}, bf16[3,3,64,32]{2,3,1,0:T(8,128)(2,1)}, u32[]{:S(2)}) copy-start(bf16[3,3,64,32]{2,3,1,0:T(8,128)(2,1)} %param.8) | copy-start | bytes 110596
  1.6 0.7 %copy-start.1 = (s32[2,16]{1,0:T(2,128)S(1)}, s32[2,16]{1,0:T(2,128)}, u32[]{:S(2)}) copy-start(s32[2,16]{1,0:T(2,128)} %labels.1) | copy-start | bytes 388
  1.7 0.7 %copy-start.2 = (f32[32]{0:T(128)S(1)}, f32[32]{0:T(128)}, u32[]{:S(2)}) copy-start(f32[32]{0:T(128)} %param.9) | copy-start | bytes 388
  1.7 0.7 %copy-start.3 = (f32[16]{0:T(128)S(1)}, f32[16]{0:T(128)}, u32[]{:S(2)}) copy-start(f32[16]{0:T(128)} %param.11) | copy-start | bytes 196
  1.7 0.7 %copy-start.4 = (f32[16]{0:T(128)S(1)}, f32[16]{0:T(128)}, u32[]{:S(2)}) copy-start(f32[16]{0:T(128)} %param.12) | copy-start | bytes 196
  2.3 1.0 %copy-start = (bf16[16,2,64,128]{3,2,1,0:T(8,128)(2,1)S(1)}, bf16[16,2,64,128]{3,2,1,0:T(8,128)(2,1)}, u32[]{:S(2)}) copy-start(bf16[16,2,64,128]{3,2,1,0:T(8,128)(2,1)} %frames.1) | copy-start | bytes 1572868

commit v2 on v1

--- a/solution.py
+++ b/solution.py
@@ -9,20 +9,19 @@
 
 MESH = pl.DeviceIdType.MESH
 CHUNK = 2
-PIECE = 32
 
 
 def fused(
     dates_n, chan_n, frames, sw, sb, tw, tb, hw, labels, logits_out, gs_out, gt_out,
-    xpad, sw_v, sb_v, tw_v, tb_v, hw_v, lab_v, wbig, hid, dact, gsh,
+    xpad, sw_v, sb_v, tw_v, tb_v, hw_v, lab_v, wbig, tw_m, hid, dact, gsh,
     lab_all, feat_all, gt_all, dwb, rs_all, ag_all,
     loc_sem, halo_send, halo_recv, fwd_send, fwd_recv, lab_send, lab_recv, feat_send, feat_recv,
     gt_send, gt_recv, rs_send, rs_recv, ag_send, ag_recv,
 ):
     f32, bf16 = jnp.float32, jnp.bfloat16
     dates, _, channels, cols = frames.shape
-    outs = sw.shape[3]
-    feats = tw.shape[2]
+    outs = sw.shape[2]
+    feats = tw.shape[1]
     half = dates // chan_n
     d, p, c = lax.axis_index("date"), lax.axis_index("pix"), lax.axis_index("chan")
 
@@ -96,13 +95,12 @@
         copy.start()
 
     xpad[:, 3 * p] = jnp.zeros((dates, channels, cols), bf16)
-    gsh[...] = jnp.zeros(gsh.shape, bf16)
     for n in range(1, 6):
         loads[n].wait()
     wbig[...] = jnp.zeros(wbig.shape, f32)
     for a in range(3):
         for b in range(3):
-            tap = sw_v[a, b].astype(f32).T
+            tap = sw_v[a, b].astype(f32)
             for i in range(2):
                 r = i + a
                 wbig[(i * 3 + b) * outs : (i * 3 + b + 1) * outs, r * channels : (r + 1) * channels] = tap
@@ -113,8 +111,9 @@
     bias_o = column(sb_v[...], outs)
     bias_f = column(tb_v[...], feats)
     head = column(hw_v[...], feats)
-    tw_m = tw_v[...].reshape(dates * outs, feats)
-    tw_t = tw_m.astype(f32).T.astype(bf16)
+    tw_f = jnp.concatenate([tw_v[t].astype(f32) for t in range(dates)], axis=1)
+    tw_t = tw_f.astype(bf16)
+    tw_m[...] = tw_f.T.astype(bf16)
     lane_o = lax.broadcasted_iota(jnp.int32, (outs, cols), 1)
     first, last = lane_o == 0, lane_o == cols - 1
 
@@ -195,17 +194,20 @@
                 g = g.astype(bf16).astype(f32)
                 at = slice((t + n) * cols, (t + n + 1) * cols)
                 for b, v in enumerate((left(g), g, right(g))):
-                    row = i * 128 + b * outs
+                    row = (i * 3 + b) * outs
                     gsh[row : row + outs, at] = v.astype(bf16)
     x_all = jnp.concatenate(
         [xpad[t].reshape(4 * channels, cols) for t in range(dates)], axis=1
     )
-    dt = lax.dot_general(x_all, gsh[...], contract, preferred_element_type=f32)
-    dwb[...] = (dt[: 3 * channels, :128] + dt[channels:, 128:]).astype(bf16)
+    dt = lax.dot_general(gsh[...], x_all, contract, preferred_element_type=f32)
+    dw = dt[: 3 * outs] + pltpu.roll(dt[3 * outs :], 3 * channels, 1)
+    for b in range(3):
+        for h in range(2):
+            dwb[2 * b + h] = dw[b * outs : (b + 1) * outs, h * 128 : (h + 1) * 128].astype(bf16)
 
     idx = d * 2 + p
     sums = dates_n * 2
-    owners = 3 * channels // PIECE
+    owners = dwb.shape[0]
     shift = (sums - owners) // 2
     mine = idx - shift
     is_owner = (mine >= 0) & (mine < owners)
@@ -213,7 +215,7 @@
     def rs_copy(k):
         to = {"date": (k + shift) // 2, "pix": (k + shift) % 2, "chan": c}
         return remote(
-            dwb.at[pl.ds(k * PIECE, PIECE)], rs_all.at[idx], rs_send.at[k], rs_recv.at[idx], to
+            dwb.at[k], rs_all.at[idx], rs_send.at[k], rs_recv.at[idx], to
         )
 
     for k in range(owners):
@@ -231,7 +233,7 @@
 
     @pl.when(is_owner)
     def _():
-        rs_all[idx] = dwb[pl.ds(pl.multiple_of(mine * PIECE, PIECE), PIECE)]
+        rs_all[idx] = dwb[mine]
         for q in range(sums):
             @pl.when(idx != q)
             def _():
@@ -241,7 +243,9 @@
             copy.start()
 
     gt_copy.wait_recv()
-    gt_out[...] = gt_all[0] + gt_all[1]
+    for t in range(dates):
+        at = slice(t * outs, (t + 1) * outs)
+        gt_out[t] = gt_all[0, :, at] + gt_all[1, :, at]
     logit_rows = jnp.concatenate(rows_out + [jnp.zeros((6, cols), f32)], axis=0)
     moved = pltpu.roll(logit_rows, lax.rem(cols - block * width, cols), 1)
     logits_out[...] = moved[:2, :width]
@@ -256,7 +260,9 @@
         @pl.when(mine != k)
         def _():
             pltpu.make_async_copy(ag_all.at[k], ag_all.at[k], ag_recv.at[k]).wait()
-        gs_out[k * PIECE : (k + 1) * PIECE] = ag_all[k].astype(f32)
+        piece = ag_all[k].astype(f32)
+        for n in range(2 - k % 2):
+            gs_out[2 * (k % 2) + n, k // 2] = piece[:, n * channels : (n + 1) * channels]
 
     @pl.when(is_owner)
     def _():
@@ -264,22 +270,32 @@
             copy.wait_send()
 
 
+def store(*refs):
+    sem = refs[6]
+    copies = [pltpu.make_async_copy(refs[i], refs[3 + i], sem.at[i]) for i in range(3)]
+    for copy in copies:
+        copy.start()
+    for copy in copies:
+        copy.wait()
+
+
 def fused_shards(dates_n, chan_n, frames, sw, sb, tw, tb, hw, labels):
     dates, rows, channels, cols = frames.shape
     outs, feats = sw.shape[3], tw.shape[2]
+    sw, tw = sw.transpose(0, 1, 3, 2), tw.transpose(0, 2, 1)
     f32, bf16 = jnp.float32, jnp.bfloat16
     steps = dates // chan_n // CHUNK
     blocks, sums = dates_n * chan_n, dates_n * 2
-    owners = 3 * channels // PIECE
+    owners = 6
     dma = pltpu.SemaphoreType.DMA
-    logits, gs, gt = pl.pallas_call(
+    made = pl.pallas_call(
         functools.partial(fused, dates_n, chan_n),
         out_shape=(
             jax.ShapeDtypeStruct(labels.shape, f32),
-            jax.ShapeDtypeStruct((3 * channels, 128), f32),
-            jax.ShapeDtypeStruct((feats, dates * outs), f32),
+            jax.ShapeDtypeStruct(sw.shape, f32),
+            jax.ShapeDtypeStruct(tw.shape, f32),
         ),
-        in_specs=[pl.BlockSpec(memory_space=pl.ANY)] * 7,
+        in_specs=[pl.BlockSpec(memory_space=pltpu.HBM)] * 7,
         out_specs=[pl.BlockSpec(memory_space=pltpu.VMEM)] * 3,
         scratch_shapes=[
             pltpu.VMEM((dates, 4, channels, cols), bf16),
@@ -290,15 +306,16 @@
             pltpu.VMEM((1, feats), f32),
             pltpu.VMEM(labels.shape, jnp.int32),
             pltpu.VMEM((6 * outs, 4 * channels), f32),
+            pltpu.VMEM((dates * outs, feats), bf16),
             pltpu.VMEM((2, dates, outs, cols), bf16),
             pltpu.VMEM((2, dates, outs, cols), f32),
-            pltpu.VMEM((256, dates * cols), bf16),
+            pltpu.VMEM((6 * outs, dates * cols), bf16),
             pltpu.VMEM((blocks, 8, cols), f32),
             pltpu.VMEM((blocks, 2 * feats, cols), bf16),
             pltpu.VMEM((2, feats, dates * outs), f32),
-            pltpu.VMEM((3 * channels, 128), bf16),
-            pltpu.VMEM((sums, PIECE, 128), bf16),
-            pltpu.VMEM((owners, PIECE, 128), bf16),
+            pltpu.VMEM((owners, outs, 128), bf16),
+            pltpu.VMEM((sums, outs, 128), bf16),
+            pltpu.VMEM((owners, outs, 128), bf16),
             dma((7,)),
             dma((steps,)),
             dma((steps,)),
@@ -316,12 +333,18 @@
             dma((owners,)),
         ],
         compiler_params=pltpu.CompilerParams(
-            collective_id=0, has_side_effects=True, vmem_limit_bytes=40 * 1024 * 1024
+            collective_id=0, has_side_effects=True, vmem_limit_bytes=56_000_000
         ),
     )(frames, sw, sb[None], tw, tb[None], hw[None], labels)
-    grad_spatial = gs[:, : 3 * outs].reshape(3, channels, 3, outs).transpose(0, 2, 1, 3)
-    grad_temporal = gt.T.reshape(dates, outs, feats)
-    return logits, grad_spatial, grad_temporal
+    logits, gs, gt = pl.pallas_call(
+        store,
+        out_shape=tuple(jax.ShapeDtypeStruct(a.shape, a.dtype) for a in made),
+        in_specs=[pl.BlockSpec(memory_space=pl.ANY)] * 3,
+        out_specs=[pl.BlockSpec(memory_space=pl.ANY)] * 3,
+        scratch_shapes=[dma((3,))],
+        compiler_params=pltpu.CompilerParams(vmem_limit_bytes=1 << 20),
+    )(*made)
+    return logits, gs.transpose(0, 1, 3, 2), gt.transpose(0, 2, 1)
 
 
 def with_halo(block, sides, width):

time: 31 us -> 29.5 us (0.952)
  local copies, waits for them, and re-layouts: 4.93 us -> 2.4 us
  Pallas kernels: 25.1 us -> 26.2 us
    unnamed x17 -> x12, local copies, waits for them, and re-layouts: 4.64 us -> 2.4 us
    pallas_call x0 -> x1, Pallas kernels: none -> 0.74 us  [fused_shards(): pl.pallas_call(store, out_shape=tuple((jax.ShapeDtypeStruct(a.shape, a.dt...]
    pallas_call x1, Pallas kernels: 25.1 us -> 25.5 us  [fused_shards(): pl.pallas_call(functools.partial(fused, dates_n, chan_n), out_shape=(jax....]
where the time goes in v2:
time: 29.5 us; the launch traced here: 29.3 us
  Pallas kernels  26.2 us (89%)
  local copies, waits for them, and re-layouts  2.4 us (8%)
  between operations  0.68 us (2%)
    pallas_call x1, Pallas kernels, fused_shards(): pl.pallas_call(functools.partial(fused, dates_n, chan_n), out_shape=(jax....  25.5 us
    unnamed x12, local copies, waits for them, and re-layouts  2.4 us
    pallas_call x1, Pallas kernels, fused_shards(): pl.pallas_call(store, out_shape=tuple((jax.ShapeDtypeStruct(a.shape, a.dt...  0.74 us

profile of v2, /device:TPU:0, one launch (start us, length us, event | category | flops | bytes accessed | tf_op | source)
XLA Modules:
  0.0 29.3 jit_solution(11279680394070616988)
XLA Ops:
  0.6 0.0 copy-start.4
  0.6 0.0 copy-start.5
  0.7 0.0 copy-start.2
  0.7 0.0 copy-start.3
  0.7 0.6 %copy-done.4 = f32[16]{0:T(128)S(1)} copy-done((f32[16]{0:T(128)S(1)}, f32[16]{0:T(128)}, u32[]{:S(2)}) %copy-start.4) | copy-done | bytes 88
  1.3 0.0 copy-done.5
  1.3 0.0 copy-done.2
  1.3 0.0 copy-done.3
  1.3 0.0 copy-start
  1.3 0.9 %copy-done = bf16[3,3,64,32]{2,3,1,0:T(8,128)(2,1)S(1)} copy-done((bf16[3,3,64,32]{2,3,1,0:T(8,128)(2,1)S(1)}, bf16[3,3,64,32]{2,3,1,0:T(8,128)(2,1)}, u32[]{:S(2)}) %copy-start) | copy-done | bytes 36888
  2.2 0.0 copy-start.1
  2.2 0.8 %copy-done.1 = bf16[16,32,16]{1,2,0:T(8,128)(2,1)S(1)} copy-done((bf16[16,32,16]{1,2,0:T(8,128)(2,1)S(1)}, bf16[16,32,16]{1,2,0:T(8,128)(2,1)}, u32[]{:S(2)}) %copy-start.1) | copy-done | bytes 16408
  3.1 25.5 %shard_map.94 = (f32[2,16]{1,0:T(2,128)S(1)}, f32[3,3,32,64]{3,2,1,0:T(8,128)S(1)}, f32[16,16,32]{2,1,0:T(8,128)S(1)}) custom-call(bf16[16,2,64,128]{3,2,1,0:T(8,128)(2,1)} %frames.1, bf16[3,3,32,64]{3,2,1,0:T(8,128)(2,1)S(1)} %bitcast.7, f32[1,32]{1,0:T(1,128)S(1)} %bitcast.9, bf16[16,16,32]{2,1,0:T(8,128)(2,1)S(1)} %bitcast.8, f32[1,16]{1,0:T(1,128)S(1)} %bitcast.10, ...), custom_call_target="tpu_custom_call" | custom-call | tf_op jit(solution)/shard_map/pallas_call | solution.py:291
  28.5 0.7 %shard_map.95 = (f32[2,16]{1,0:T(2,128)}, f32[3,3,32,64]{3,2,1,0:T(8,128)}, f32[16,16,32]{2,1,0:T(8,128)}) custom-call(f32[2,16]{1,0:T(2,128)S(1)} %get-tuple-element.9.refs_0_, f32[3,3,32,64]{3,2,1,0:T(8,128)S(1)} %get-tuple-element.10.refs_1_, f32[16,16,32]{2,1,0:T(8,128)S(1)} %get-tuple-element.11.refs_2_), custom_call_target="tpu_custom_call" | custom-call | tf_op jit(solution)/shard_map/pallas_call | solution.py:339
Async XLA Ops:
  0.6 0.7 %copy-start.4 = (f32[16]{0:T(128)S(1)}, f32[16]{0:T(128)}, u32[]{:S(2)}) copy-start(f32[16]{0:T(128)} %param.11) | copy-start | bytes 196
  0.6 0.7 %copy-start.5 = (f32[16]{0:T(128)S(1)}, f32[16]{0:T(128)}, u32[]{:S(2)}) copy-start(f32[16]{0:T(128)} %param.12) | copy-start | bytes 196
  0.7 0.7 %copy-start.2 = (s32[2,16]{1,0:T(2,128)S(1)}, s32[2,16]{1,0:T(2,128)}, u32[]{:S(2)}) copy-start(s32[2,16]{1,0:T(2,128)} %labels.1) | copy-start | bytes 388
  0.7 0.7 %copy-start.3 = (f32[32]{0:T(128)S(1)}, f32[32]{0:T(128)}, u32[]{:S(2)}) copy-start(f32[32]{0:T(128)} %param.9) | copy-start | bytes 388
  1.3 0.9 %copy-start = (bf16[3,3,64,32]{2,3,1,0:T(8,128)(2,1)S(1)}, bf16[3,3,64,32]{2,3,1,0:T(8,128)(2,1)}, u32[]{:S(2)}) copy-start(bf16[3,3,64,32]{2,3,1,0:T(8,128)(2,1)} %param.8) | copy-start | bytes 110596
  2.2 0.8 %copy-start.1 = (bf16[16,32,16]{1,2,0:T(8,128)(2,1)S(1)}, bf16[16,32,16]{1,2,0:T(8,128)(2,1)}, u32[]{:S(2)}) copy-start(bf16[16,32,16]{1,2,0:T(8,128)(2,1)} %param.10) | copy-start | bytes 49156

commit v3 on v2

--- a/solution.py
+++ b/solution.py
@@ -8,7 +8,7 @@
 from jax.sharding import PartitionSpec as P
 
 MESH = pl.DeviceIdType.MESH
-CHUNK = 2
+CHUNK = 8
 
 
 def fused(
@@ -178,11 +178,6 @@
     fgrad = jnp.concatenate(grads, axis=1)
 
     contract = (((1,), (1,)), ((), ()))
-    gt_all[p] = lax.dot_general(
-        fgrad, jnp.concatenate(hid_m, axis=1), contract, preferred_element_type=f32
-    )
-    gt_copy = remote(gt_all.at[p], gt_all.at[p], gt_send, gt_recv, target(0, 1, 0))
-    gt_copy.start()
 
     for t in range(0, dates, CHUNK):
         hgrad = jnp.dot(
@@ -223,6 +218,12 @@
         def _():
             rs_copy(k).start()
 
+    gt_all[p] = lax.dot_general(
+        fgrad, jnp.concatenate(hid_m, axis=1), contract, preferred_element_type=f32
+    )
+    gt_copy = remote(gt_all.at[p], gt_all.at[p], gt_send, gt_recv, target(0, 1, 0))
+    gt_copy.start()
+
     all_other = [(od, op) for od in reversed(range(dates_n)) for op in reversed(range(2)) if od or op]
 
     def ag_copies():
@@ -243,9 +244,7 @@
             copy.start()
 
     gt_copy.wait_recv()
-    for t in range(dates):
-        at = slice(t * outs, (t + 1) * outs)
-        gt_out[t] = gt_all[0, :, at] + gt_all[1, :, at]
+    gt_out[...] = gt_all[0] + gt_all[1]
     logit_rows = jnp.concatenate(rows_out + [jnp.zeros((6, cols), f32)], axis=0)
     moved = pltpu.roll(logit_rows, lax.rem(cols - block * width, cols), 1)
     logits_out[...] = moved[:2, :width]
@@ -260,9 +259,7 @@
         @pl.when(mine != k)
         def _():
             pltpu.make_async_copy(ag_all.at[k], ag_all.at[k], ag_recv.at[k]).wait()
-        piece = ag_all[k].astype(f32)
-        for n in range(2 - k % 2):
-            gs_out[2 * (k % 2) + n, k // 2] = piece[:, n * channels : (n + 1) * channels]
+        gs_out[k] = ag_all[k]
 
     @pl.when(is_owner)
     def _():
@@ -270,13 +267,16 @@
             copy.wait_send()
 
 
-def store(*refs):
-    sem = refs[6]
-    copies = [pltpu.make_async_copy(refs[i], refs[3 + i], sem.at[i]) for i in range(3)]
-    for copy in copies:
-        copy.start()
-    for copy in copies:
-        copy.wait()
+def unpack(logits, gs, gt, logits_out, gs_out, gt_out):
+    channels = gs_out.shape[3]
+    outs = gt_out.shape[2]
+    logits_out[...] = logits[...]
+    for k in range(gs.shape[0]):
+        piece = gs[k].astype(jnp.float32)
+        for n in range(2 - k % 2):
+            gs_out[2 * (k % 2) + n, k // 2] = piece[:, n * channels : (n + 1) * channels]
+    for t in range(gt_out.shape[0]):
+        gt_out[t] = gt[:, t * outs : (t + 1) * outs]
 
 
 def fused_shards(dates_n, chan_n, frames, sw, sb, tw, tb, hw, labels):
@@ -292,8 +292,8 @@
         functools.partial(fused, dates_n, chan_n),
         out_shape=(
             jax.ShapeDtypeStruct(labels.shape, f32),
-            jax.ShapeDtypeStruct(sw.shape, f32),
-            jax.ShapeDtypeStruct(tw.shape, f32),
+            jax.ShapeDtypeStruct((owners, outs, 128), bf16),
+            jax.ShapeDtypeStruct((feats, dates * outs), f32),
         ),
         in_specs=[pl.BlockSpec(memory_space=pltpu.HBM)] * 7,
         out_specs=[pl.BlockSpec(memory_space=pltpu.VMEM)] * 3,
@@ -333,15 +333,14 @@
             dma((owners,)),
         ],
         compiler_params=pltpu.CompilerParams(
-            collective_id=0, has_side_effects=True, vmem_limit_bytes=56_000_000
+            collective_id=0, has_side_effects=True, vmem_limit_bytes=56_400_000
         ),
     )(frames, sw, sb[None], tw, tb[None], hw[None], labels)
     logits, gs, gt = pl.pallas_call(
-        store,
-        out_shape=tuple(jax.ShapeDtypeStruct(a.shape, a.dtype) for a in made),
-        in_specs=[pl.BlockSpec(memory_space=pl.ANY)] * 3,
-        out_specs=[pl.BlockSpec(memory_space=pl.ANY)] * 3,
-        scratch_shapes=[dma((3,))],
+        unpack,
+        out_shape=tuple(jax.ShapeDtypeStruct(shape, f32) for shape in (labels.shape, sw.shape, tw.shape)),
+        in_specs=[pl.BlockSpec(memory_space=pltpu.VMEM)] * 3,
+        out_specs=[pl.BlockSpec(memory_space=pltpu.VMEM)] * 3,
         compiler_params=pltpu.CompilerParams(vmem_limit_bytes=1 << 20),
     )(*made)
     return logits, gs.transpose(0, 1, 3, 2), gt.transpose(0, 2, 1)

time: 29.5 us -> 27 us (0.915)
  local copies, waits for them, and re-layouts: 2.4 us -> 0.68 us
  Pallas kernels: 26.2 us -> 25.5 us
    unnamed x12 -> x8, local copies, waits for them, and re-layouts: 2.4 us -> 0.68 us
    pallas_call x1, Pallas kernels: 25.5 us -> 24.7 us  [fused_shards(): pl.pallas_call(functools.partial(fused, dates_n, chan_n), out_shape=(jax....]
where the time goes in v3:
time: 27 us; the launch traced here: 26.8 us
  Pallas kernels  25.5 us (94%)
  local copies, waits for them, and re-layouts  0.68 us (3%)
  between operations  0.67 us (2%)
    pallas_call x1, Pallas kernels, fused_shards(): pl.pallas_call(functools.partial(fused, dates_n, chan_n), out_shape=(jax....  24.7 us
    pallas_call x1, Pallas kernels, fused_shards(): pl.pallas_call(unpack, out_shape=tuple((jax.ShapeDtypeStruct(shape, f32)...  0.78 us
    unnamed x8, local copies, waits for them, and re-layouts  0.68 us

profile of v3, /device:TPU:0, one launch (start us, length us, event | category | flops | bytes accessed | tf_op | source)
XLA Modules:
  0.0 26.8 jit_solution(4365188208771999322)
XLA Ops:
  0.6 0.0 copy-start.2
  0.6 0.0 copy-start.3
  0.7 0.0 copy-start
  0.7 0.0 copy-start.1
  0.7 0.6 %copy-done.2 = f32[16]{0:T(128)S(1)} copy-done((f32[16]{0:T(128)S(1)}, f32[16]{0:T(128)}, u32[]{:S(2)}) %copy-start.2) | copy-done | bytes 88
  1.3 0.0 copy-done.3
  1.3 0.0 copy-done
  1.3 0.0 copy-done.1
  1.3 24.7 %shard_map.94 = (f32[2,16]{1,0:T(2,128)S(1)}, bf16[6,32,128]{2,1,0:T(8,128)(2,1)S(1)}, f32[16,512]{1,0:T(8,128)S(1)}) custom-call(bf16[16,2,64,128]{3,2,1,0:T(8,128)(2,1)} %frames.1, bf16[3,3,32,64]{3,2,1,0:T(8,128)(2,1)} %bitcast.10, f32[1,32]{1,0:T(1,128)S(1)} %bitcast.7, bf16[16,16,32]{2,1,0:T(8,128)(2,1)} %bitcast.11, f32[1,16]{1,0:T(1,128)S(1)} %bitcast.8, ...), custom_call_target="tpu_custom_call" | custom-call | tf_op jit(solution)/shard_map/pallas_call | solution.py:291
  26.0 0.8 %shard_map.95 = (f32[2,16]{1,0:T(2,128)}, f32[3,3,32,64]{3,2,1,0:T(8,128)}, f32[16,16,32]{2,1,0:T(8,128)}) custom-call(f32[2,16]{1,0:T(2,128)S(1)} %get-tuple-element.9.logits, bf16[6,32,128]{2,1,0:T(8,128)(2,1)S(1)} %get-tuple-element.10.gs, f32[16,512]{1,0:T(8,128)S(1)} %get-tuple-element.11.gt), custom_call_target="tpu_custom_call" | custom-call | tf_op jit(solution)/shard_map/pallas_call | solution.py:339
Async XLA Ops:
  0.6 0.7 %copy-start.2 = (f32[16]{0:T(128)S(1)}, f32[16]{0:T(128)}, u32[]{:S(2)}) copy-start(f32[16]{0:T(128)} %param.11) | copy-start | bytes 196
  0.6 0.7 %copy-start.3 = (f32[16]{0:T(128)S(1)}, f32[16]{0:T(128)}, u32[]{:S(2)}) copy-start(f32[16]{0:T(128)} %param.12) | copy-start | bytes 196
  0.7 0.7 %copy-start = (s32[2,16]{1,0:T(2,128)S(1)}, s32[2,16]{1,0:T(2,128)}, u32[]{:S(2)}) copy-start(s32[2,16]{1,0:T(2,128)} %labels.1) | copy-start | bytes 388
  0.7 0.7 %copy-start.1 = (f32[32]{0:T(128)S(1)}, f32[32]{0:T(128)}, u32[]{:S(2)}) copy-start(f32[32]{0:T(128)} %param.9) | copy-start | bytes 388

commit v4 on v3

--- a/solution.py
+++ b/solution.py
@@ -97,13 +97,10 @@
     xpad[:, 3 * p] = jnp.zeros((dates, channels, cols), bf16)
     for n in range(1, 6):
         loads[n].wait()
-    wbig[...] = jnp.zeros(wbig.shape, f32)
     for a in range(3):
         for b in range(3):
             tap = sw_v[a, b].astype(f32)
-            for i in range(2):
-                r = i + a
-                wbig[(i * 3 + b) * outs : (i * 3 + b + 1) * outs, r * channels : (r + 1) * channels] = tap
+            wbig[b * outs : (b + 1) * outs, a * channels : (a + 1) * channels] = tap
     conv = wbig[...].astype(bf16)
     def column(row, n):
         same = lax.broadcasted_iota(jnp.int32, (n, n), 0) == lax.broadcasted_iota(jnp.int32, (n, n), 1)
@@ -123,53 +120,57 @@
     def left(x):
         return jnp.where(last, 0.0, pltpu.roll(x, cols - 1, 1))
 
-    def forward(start):
-        x = xpad[pl.ds(start, CHUNK)].reshape(CHUNK, 4 * channels, cols)
+    def forward(start, row):
+        x = xpad[pl.ds(start, CHUNK), pl.ds(row, 3)].reshape(CHUNK, 3 * channels, cols)
         z = jnp.dot(
             conv, jnp.concatenate([x[n] for n in range(CHUNK)], axis=1), preferred_element_type=f32
         )
         for n in range(CHUNK):
-            for i in range(2):
-                tap = [
-                    z[(i * 3 + b) * outs : (i * 3 + b + 1) * outs, n * cols : (n + 1) * cols] for b in range(3)
-                ]
-                pre = tap[1] + right(tap[0]) + left(tap[2]) + bias_o
-                sig = jax.nn.sigmoid(pre)
-                hid[i, start + n] = (pre * sig).astype(bf16)
-                dact[i, start + n] = sig * (1.0 + pre * (1.0 - sig))
+            tap = [z[b * outs : (b + 1) * outs, n * cols : (n + 1) * cols] for b in range(3)]
+            pre = tap[1] + right(tap[0]) + left(tap[2]) + bias_o
+            sig = jax.nn.sigmoid(pre)
+            hid[row, start + n] = (pre * sig).astype(bf16)
+            dact[row, start + n] = sig * (1.0 + pre * (1.0 - sig))
+
+    def spread_partial(step, row):
+        part = jnp.dot(tw_t, hid[row].reshape(dates * outs, cols), preferred_element_type=f32)
+        feat_all[row, block] = part.astype(bf16)
+        mine = feat_all.at[row, block]
+        copies = [
+            remote(mine, mine, feat_send.at[step, n], feat_recv.at[step, n], target(od, 0, oc))
+            for n, (od, oc) in enumerate(group)
+        ]
+        for copy in copies:
+            copy.start()
+        return copies
 
     loads[0].wait()
+    for t in range(0, dates, CHUNK):
+        forward(t, p)
+    feat_copies = spread_partial(0, p)
+
     other = 1 - c
     steps = half // CHUNK
     for k in range(steps):
         halo[k].wait_recv()
         passed[k].start()
-        forward(c * half + k * CHUNK)
+        forward(c * half + k * CHUNK, 1 - p)
         if k:
             passed[k - 1].wait_recv()
-            forward(other * half + (k - 1) * CHUNK)
+            forward(other * half + (k - 1) * CHUNK, 1 - p)
     passed[steps - 1].wait_recv()
-    forward(other * half + (steps - 1) * CHUNK)
-
-    hid_m = [hid[i].reshape(dates * outs, cols) for i in range(2)]
-    part = jnp.concatenate([jnp.dot(tw_t, hid_m[i], preferred_element_type=f32) for i in range(2)], axis=0)
-    feat_all[block] = part.astype(bf16)
-    feat_copies = [
-        remote(feat_all.at[block], feat_all.at[block], feat_send.at[n], feat_recv.at[n], target(od, 0, oc))
-        for n, (od, oc) in enumerate(group)
-    ]
-    for copy in feat_copies:
-        copy.start()
+    forward(other * half + (steps - 1) * CHUNK, 1 - p)
+    feat_copies += spread_partial(1, 1 - p)
+
     for copy in lab_copies:
         copy.wait_recv()
     lab = jnp.sum(lab_all[...], axis=0)
     for copy in feat_copies:
         copy.wait_recv()
-    total = jnp.sum(feat_all[...].astype(f32), axis=0)
 
     grads, rows_out = [], []
     for i in range(2):
-        feature = total[i * feats : (i + 1) * feats] + bias_f
+        feature = jnp.sum(feat_all[i].astype(f32), axis=0) + bias_f
         sig = jax.nn.sigmoid(feature)
         logit = jnp.sum(feature * sig * head, axis=0, keepdims=True)
         dlogit = jax.nn.sigmoid(logit) - lab[i : i + 1]
@@ -219,7 +220,7 @@
             rs_copy(k).start()
 
     gt_all[p] = lax.dot_general(
-        fgrad, jnp.concatenate(hid_m, axis=1), contract, preferred_element_type=f32
+        fgrad, jnp.concatenate([hid[i].reshape(dates * outs, cols) for i in range(2)], axis=1), contract, preferred_element_type=f32
     )
     gt_copy = remote(gt_all.at[p], gt_all.at[p], gt_send, gt_recv, target(0, 1, 0))
     gt_copy.start()
@@ -305,13 +306,13 @@
             pltpu.VMEM((1, feats), f32),
             pltpu.VMEM((1, feats), f32),
             pltpu.VMEM(labels.shape, jnp.int32),
-            pltpu.VMEM((6 * outs, 4 * channels), f32),
+            pltpu.VMEM((3 * outs, 3 * channels), f32),
             pltpu.VMEM((dates * outs, feats), bf16),
             pltpu.VMEM((2, dates, outs, cols), bf16),
             pltpu.VMEM((2, dates, outs, cols), f32),
             pltpu.VMEM((6 * outs, dates * cols), bf16),
             pltpu.VMEM((blocks, 8, cols), f32),
-            pltpu.VMEM((blocks, 2 * feats, cols), bf16),
+            pltpu.VMEM((2, blocks, feats, cols), bf16),
             pltpu.VMEM((2, feats, dates * outs), f32),
             pltpu.VMEM((owners, outs, 128), bf16),
             pltpu.VMEM((sums, outs, 128), bf16),
@@ -323,8 +324,8 @@
             dma((steps,)),
             dma((blocks,)),
             dma((blocks,)),
-            dma((blocks,)),
-            dma((blocks,)),
+            dma((2, blocks)),
+            dma((2, blocks)),
             dma,
             dma,
             dma((owners,)),

time: 27 us -> 26.3 us (0.974)
  Pallas kernels: 25.5 us -> 24.8 us
    pallas_call x1, Pallas kernels: 24.7 us -> 24 us  [fused_shards(): pl.pallas_call(functools.partial(fused, dates_n, chan_n), out_shape=(jax....]
where the time goes in v4:
time: 26.3 us; the launch traced here: 26.2 us
  Pallas kernels  24.8 us (94%)
  local copies, waits for them, and re-layouts  0.68 us (3%)
  between operations  0.67 us (3%)
    pallas_call x1, Pallas kernels, fused_shards(): pl.pallas_call(functools.partial(fused, dates_n, chan_n), out_shape=(jax....  24 us
    pallas_call x1, Pallas kernels, fused_shards(): pl.pallas_call(unpack, out_shape=tuple((jax.ShapeDtypeStruct(shape, f32)...  0.78 us
    unnamed x8, local copies, waits for them, and re-layouts  0.68 us

profile of v4, /device:TPU:0, one launch (start us, length us, event | category | flops | bytes accessed | tf_op | source)
XLA Modules:
  0.0 26.2 jit_solution(7405886315031324332)
XLA Ops:
  0.6 0.0 copy-start.2
  0.6 0.0 copy-start.3
  0.7 0.0 copy-start
  0.7 0.0 copy-start.1
  0.7 0.6 %copy-done.2 = f32[16]{0:T(128)S(1)} copy-done((f32[16]{0:T(128)S(1)}, f32[16]{0:T(128)}, u32[]{:S(2)}) %copy-start.2) | copy-done | bytes 88
  1.3 0.0 copy-done.3
  1.3 0.0 copy-done
  1.3 0.0 copy-done.1
  1.3 24.0 %shard_map.94 = (f32[2,16]{1,0:T(2,128)S(1)}, bf16[6,32,128]{2,1,0:T(8,128)(2,1)S(1)}, f32[16,512]{1,0:T(8,128)S(1)}) custom-call(bf16[16,2,64,128]{3,2,1,0:T(8,128)(2,1)} %frames.1, bf16[3,3,32,64]{3,2,1,0:T(8,128)(2,1)} %bitcast.10, f32[1,32]{1,0:T(1,128)S(1)} %bitcast.7, bf16[16,16,32]{2,1,0:T(8,128)(2,1)} %bitcast.11, f32[1,16]{1,0:T(1,128)S(1)} %bitcast.8, ...), custom_call_target="tpu_custom_call" | custom-call | tf_op jit(solution)/shard_map/pallas_call | solution.py:292
  25.4 0.8 %shard_map.95 = (f32[2,16]{1,0:T(2,128)}, f32[3,3,32,64]{3,2,1,0:T(8,128)}, f32[16,16,32]{2,1,0:T(8,128)}) custom-call(f32[2,16]{1,0:T(2,128)S(1)} %get-tuple-element.9.logits, bf16[6,32,128]{2,1,0:T(8,128)(2,1)S(1)} %get-tuple-element.10.gs, f32[16,512]{1,0:T(8,128)S(1)} %get-tuple-element.11.gt), custom_call_target="tpu_custom_call" | custom-call | tf_op jit(solution)/shard_map/pallas_call | solution.py:340
Async XLA Ops:
  0.6 0.7 %copy-start.2 = (f32[16]{0:T(128)S(1)}, f32[16]{0:T(128)}, u32[]{:S(2)}) copy-start(f32[16]{0:T(128)} %param.11) | copy-start | bytes 196
  0.6 0.7 %copy-start.3 = (f32[16]{0:T(128)S(1)}, f32[16]{0:T(128)}, u32[]{:S(2)}) copy-start(f32[16]{0:T(128)} %param.12) | copy-start | bytes 196
  0.7 0.7 %copy-start = (s32[2,16]{1,0:T(2,128)S(1)}, s32[2,16]{1,0:T(2,128)}, u32[]{:S(2)}) copy-start(s32[2,16]{1,0:T(2,128)} %labels.1) | copy-start | bytes 388
  0.7 0.7 %copy-start.1 = (f32[32]{0:T(128)S(1)}, f32[32]{0:T(128)}, u32[]{:S(2)}) copy-start(f32[32]{0:T(128)} %param.9) | copy-start | bytes 388

commit v5 on v4

--- a/solution.py
+++ b/solution.py
@@ -41,8 +41,8 @@
     partners = [
         (od, op, oc)
         for od in range(dates_n)
+        for oc in range(chan_n)
         for op in range(2)
-        for oc in range(chan_n)
         if (od or op or oc) and not (op and oc)
     ]
     for offs in partners:
@@ -198,8 +198,10 @@
     dt = lax.dot_general(gsh[...], x_all, contract, preferred_element_type=f32)
     dw = dt[: 3 * outs] + pltpu.roll(dt[3 * outs :], 3 * channels, 1)
     for b in range(3):
-        for h in range(2):
-            dwb[2 * b + h] = dw[b * outs : (b + 1) * outs, h * 128 : (h + 1) * 128].astype(bf16)
+        dwb[b] = dw[b * outs : (b + 1) * outs, :128].astype(bf16)
+    rest = [dw[b * outs : (b + 1) * outs, 128:192] for b in range(3)]
+    dwb[3] = jnp.concatenate(rest[:2], axis=1).astype(bf16)
+    dwb[4] = jnp.concatenate([rest[2], jnp.zeros_like(rest[2])], axis=1).astype(bf16)
 
     idx = d * 2 + p
     sums = dates_n * 2
@@ -274,8 +276,9 @@
     logits_out[...] = logits[...]
     for k in range(gs.shape[0]):
         piece = gs[k].astype(jnp.float32)
-        for n in range(2 - k % 2):
-            gs_out[2 * (k % 2) + n, k // 2] = piece[:, n * channels : (n + 1) * channels]
+        for n in range(2 if k < 4 else 1):
+            a, b = (n, k) if k < 3 else (2, 2 * (k - 3) + n)
+            gs_out[a, b] = piece[:, n * channels : (n + 1) * channels]
     for t in range(gt_out.shape[0]):
         gt_out[t] = gt[:, t * outs : (t + 1) * outs]
 
@@ -287,7 +290,7 @@
     f32, bf16 = jnp.float32, jnp.bfloat16
     steps = dates // chan_n // CHUNK
     blocks, sums = dates_n * chan_n, dates_n * 2
-    owners = 6
+    owners = 5
     dma = pltpu.SemaphoreType.DMA
     made = pl.pallas_call(
         functools.partial(fused, dates_n, chan_n),

time: 26.3 us -> 26.4 us (level)
  no operation moved by 1% of the time
where the time goes in v5:
time: 26.4 us; the launch traced here: 26.2 us
  Pallas kernels  24.9 us (94%)
  local copies, waits for them, and re-layouts  0.68 us (3%)
  between operations  0.67 us (3%)
    pallas_call x1, Pallas kernels, fused_shards(): pl.pallas_call(functools.partial(fused, dates_n, chan_n), out_shape=(jax....  24.1 us
    pallas_call x1, Pallas kernels, fused_shards(): pl.pallas_call(unpack, out_shape=tuple((jax.ShapeDtypeStruct(shape, f32)...  0.78 us
    unnamed x8, local copies, waits for them, and re-layouts  0.68 us

profile of v5, /device:TPU:0, one launch (start us, length us, event | category | flops | bytes accessed | tf_op | source)
XLA Modules:
  0.0 26.2 jit_solution(4655428052426046839)
XLA Ops:
  0.6 0.0 copy-start.2
  0.6 0.0 copy-start.3
  0.7 0.0 copy-start
  0.7 0.0 copy-start.1
  0.7 0.6 %copy-done.2 = f32[16]{0:T(128)S(1)} copy-done((f32[16]{0:T(128)S(1)}, f32[16]{0:T(128)}, u32[]{:S(2)}) %copy-start.2) | copy-done | bytes 88
  1.3 0.0 copy-done.3
  1.3 0.0 copy-done
  1.3 0.0 copy-done.1
  1.3 24.1 %shard_map.94 = (f32[2,16]{1,0:T(2,128)S(1)}, bf16[5,32,128]{2,1,0:T(8,128)(2,1)S(1)}, f32[16,512]{1,0:T(8,128)S(1)}) custom-call(bf16[16,2,64,128]{3,2,1,0:T(8,128)(2,1)} %frames.1, bf16[3,3,32,64]{3,2,1,0:T(8,128)(2,1)} %bitcast.10, f32[1,32]{1,0:T(1,128)S(1)} %bitcast.7, bf16[16,16,32]{2,1,0:T(8,128)(2,1)} %bitcast.11, f32[1,16]{1,0:T(1,128)S(1)} %bitcast.8, ...), custom_call_target="tpu_custom_call" | custom-call | tf_op jit(solution)/shard_map/pallas_call | solution.py:295
  25.4 0.8 %shard_map.95 = (f32[2,16]{1,0:T(2,128)}, f32[3,3,32,64]{3,2,1,0:T(8,128)}, f32[16,16,32]{2,1,0:T(8,128)}) custom-call(f32[2,16]{1,0:T(2,128)S(1)} %get-tuple-element.9.logits, bf16[5,32,128]{2,1,0:T(8,128)(2,1)S(1)} %get-tuple-element.10.gs, f32[16,512]{1,0:T(8,128)S(1)} %get-tuple-element.11.gt), custom_call_target="tpu_custom_call" | custom-call | tf_op jit(solution)/shard_map/pallas_call | solution.py:343
Async XLA Ops:
  0.6 0.7 %copy-start.2 = (f32[16]{0:T(128)S(1)}, f32[16]{0:T(128)}, u32[]{:S(2)}) copy-start(f32[16]{0:T(128)} %param.11) | copy-start | bytes 196
  0.6 0.7 %copy-start.3 = (f32[16]{0:T(128)S(1)}, f32[16]{0:T(128)}, u32[]{:S(2)}) copy-start(f32[16]{0:T(128)} %param.12) | copy-start | bytes 196
  0.7 0.7 %copy-start = (s32[2,16]{1,0:T(2,128)S(1)}, s32[2,16]{1,0:T(2,128)}, u32[]{:S(2)}) copy-start(s32[2,16]{1,0:T(2,128)} %labels.1) | copy-start | bytes 388
  0.7 0.7 %copy-start.1 = (f32[32]{0:T(128)S(1)}, f32[32]{0:T(128)}, u32[]{:S(2)}) copy-start(f32[32]{0:T(128)} %param.9) | copy-start | bytes 388
